TPU v7x, 128 devices: a whole 4x4x4 slice. The times are simulated.
128 devices in a mesh: depth: 4 (over z_lo, core), row: 8 (over y, z_hi), col: 4 (over x).
Axes of the slice: x: 4, y: 4, z: 4 (z_hi: 2, z_lo: 2; z = z_hi * 2 + z_lo), core: 2. Of those that a mesh axis runs over, the one named last changes fastest.
Arguments:
- inputs: bfloat16 [1536, 12288], P(('depth', 'row'), 'col'), may hold values from -1.5 to 1.5
- weight: bfloat16 [12288, 24576], P('col', ('depth', 'row')), may hold values from -0.0390625 to 0.0390625
- pre_act: bfloat16 [1536, 24576], P('col', ('depth', 'row')), may hold values from -6 to 6
- grad_hidden: bfloat16 [1536, 24576], P('col', ('depth', 'row')), may hold values from -6 to 6
Outputs:
- grad_inputs: bfloat16 [1536, 12288], P(('depth', 'row'), 'col')
- grad_weight: bfloat16 [12288, 24576], P('col', ('depth', 'row'))
All inputs are finite; a program needn't handle non-finite values.
Results may differ from a plain program's by a relative error of at most 0.005.
Values may be sent and summed in bfloat16 or wider, within the bound.
A program may use at most 128 MiB of HBM per device.

v0:
```python
import math

import jax
import jax.numpy as jnp
from jax import lax
from jax.sharding import PartitionSpec as P


def gelu_slope(pre):
    coeff = math.sqrt(2.0 / math.pi)
    inner = coeff * (pre + 0.044715 * pre * pre * pre)
    tanh_val = jnp.tanh(inner)
    return 0.5 * (1.0 + tanh_val) + 0.5 * pre * (1.0 - tanh_val * tanh_val) * coeff * (
        1.0 + 3.0 * 0.044715 * pre * pre
    )


def per_device(inputs, weight, pre_act, grad_hidden):
    slope = gelu_slope(pre_act.astype(jnp.float32))
    grad_pre = (grad_hidden.astype(jnp.float32) * slope).astype(jnp.bfloat16)
    grad_all = lax.all_gather(grad_pre, "col", axis=0, tiled=True)
    rows = grad_all
    total = lax.dot_general(
        lax.all_gather(inputs, ("depth", "row"), axis=0, tiled=True),
        rows,
        (((0,), (0,)), ((), ())),
        preferred_element_type=jnp.float32,
    )
    grad_weight = total.astype(jnp.bfloat16)
    rows = grad_all
    summed = lax.psum_scatter(
        lax.dot_general(rows, weight, (((1,), (1,)), ((), ())), preferred_element_type=jnp.float32),
        ("depth", "row"),
        scatter_dimension=0,
        tiled=True,
    )
    grad_inputs = summed.astype(jnp.bfloat16)
    return (grad_inputs, grad_weight)


def solution(mesh):
    return jax.shard_map(
        per_device,
        mesh=mesh,
        in_specs=(
            P(("depth", "row"), "col"),
            P("col", ("depth", "row")),
            P("col", ("depth", "row")),
            P("col", ("depth", "row")),
        ),
        out_specs=(P(("depth", "row"), "col"), P("col", ("depth", "row"))),
        check_vma=False,
    )
```

profile of v0, /device:TPU:1, one launch (start us, length us, event | category | flops | bytes accessed | tf_op | source)
XLA Modules:
  0.0 559.2 jit_solution(11405904349701017644)
XLA Ops:
  7.2 0.0 all-gather.3.cloned.1.call-start
  7.2 2.9 fusion.8
  10.1 0.0 all-gather.3.cloned.1.call-update
  10.1 0.0 all-gather.5.cloned.1.call-start
  10.2 0.7 all-gather.5.cloned.1.call-update
  10.9 0.0 reduce-scatter.2.cloned.1.call-start
  10.9 35.5 %all-gather.3.cloned.1.call-done = bf16[1536,768]{1,0:T(8,128)(2,1)} async-done(((bf16[384,768]{1,0:T(8,128)(2,1)}), bf16[1536,768]{1,0:T(8,128)(2,1)}) %all-gather.3.cloned.1.call-update) | async-done | bytes 2359312 | tf_op jit(solution)/shard_map/all_gather | solution.py:21
  46.5 13.8 %fusion.10 = f32[1536,3072]{1,0:T(8,128)} fusion(bf16[1536,768]{1,0:T(8,128)(2,1)} %all-gather.3.cloned.1.call-done, bf16[3072,768]{1,0:T(8,128)(2,1)} %param.5), kind=kOutput, calls=%fused_computation.18 | convolution fusion | flops 7247757312 | bytes 25952256 | tf_op jit(solution)/shard_map/dot_general | solution.py:32
  60.3 0.0 copy-start
  60.3 0.0 reduce-scatter.2.cloned.1.call-update
  60.3 82.0 %all-gather.5.cloned.1.call-done = bf16[1536,3072]{1,0:T(8,128)(2,1)} async-done(((bf16[48,3072]{1,0:T(8,128)(2,1)}), bf16[1536,3072]{1,0:T(8,128)(2,1)}) %all-gather.5.cloned.1.call-update) | async-done | bytes 9437200 | tf_op jit(solution)/shard_map/all_gather | solution.py:24
  142.4 0.0 copy-done
  142.4 12.9 %fusion = bf16[3072,768]{0,1:T(8,128)(2,1)} fusion(bf16[1536,768]{1,0:T(8,128)(2,1)S(1)} %copy-done, bf16[1536,3072]{1,0:T(8,128)(2,1)} %all-gather.5.cloned.1.call-done), kind=kOutput, calls=%fused_computation.1 | convolution fusion | flops 7250116608 | bytes 16515072 | tf_op jit(solution)/shard_map/dot_general | solution.py:23
  155.3 6.6 %copy.6 = bf16[3072,768]{1,0:T(8,128)(2,1)} copy(bf16[3072,768]{0,1:T(8,128)(2,1)} %fusion) | data formatting | bytes 9437184
  161.9 389.0 %reduce-scatter.2.cloned.1.call-done = f32[48,3072]{1,0:T(8,128)} async-done(((f32[1536,3072]{1,0:T(8,128)}), f32[48,3072]{1,0:T(8,128)}) %reduce-scatter.2.cloned.1.call-update) | async-done | bytes 589840 | tf_op jit(solution)/shard_map/reduce_scatter | solution.py:31
  550.9 1.8 convert_element_type.21
Async XLA Ops:
  7.2 39.3 %all-gather.3.cloned.1.call-start = ((), (), s32[]{:S(2)}) async-start(), calls=%async_computation.1 | async-start | bytes 2949120 | tf_op jit(solution)/shard_map/all_gather | solution.py:21
  10.1 132.3 %all-gather.5.cloned.1.call-start = ((), (), s32[]{:S(2)}) async-start(), calls=%async_computation.3 | async-start | bytes 9732096 | tf_op jit(solution)/shard_map/all_gather | solution.py:24
  10.9 540.0 %reduce-scatter.2.cloned.1.call-start = ((), (), s32[]{:S(2)}) async-start(), calls=%async_computation.2 | async-start | bytes 19464192 | tf_op jit(solution)/shard_map/reduce_scatter | solution.py:31
  60.3 82.1 %copy-start = (bf16[1536,768]{1,0:T(8,128)(2,1)S(1)}, bf16[1536,768]{1,0:T(8,128)(2,1)}, u32[]{:S(2)}) copy-start(bf16[1536,768]{1,0:T(8,128)(2,1)} %all-gather.3.cloned.1.call-done) | copy-start | bytes 7077892
Sparse Core Ops, SparseCore 0:
  10.2 36.1 all-gather.2
  48.1 94.2 all-gather.4
  144.8 406.0 reduce-scatter.1
where the time goes:
time: 560 us; the launch traced here: 559 us
  waiting for transfers between devices  507 us (91%)
  matrix products  26.7 us (5%)
  between operations  13.7 us (2%)
  local copies, waits for them, and re-layouts  6.63 us (1%)
    reduce_scatter x1, waiting for transfers between devices, per_device(): lax.psum_scatter(lax.dot_general(rows, weight, (((1,), (1,)), ((), ())),...  389 us
    all_gather x1, waiting for transfers between devices, per_device(): lax.all_gather(inputs, ('depth', 'row'), axis=0, tiled=True)  82 us
    all_gather x1, waiting for transfers between devices, per_device(): grad_all = lax.all_gather(grad_pre, 'col', axis=0, tiled=True)  35.5 us
    dot_general x1, matrix products, per_device(): lax.dot_general(rows, weight, (((1,), (1,)), ((), ())), preferred_element...  13.8 us
    dot_general x1, matrix products, per_device(): lax.dot_general(lax.all_gather(inputs, ('depth', 'row'), axis=0, tiled=Tr...  12.9 us
  transfers between devices with their start and end apart: 3, of which 3 were waited for; matrix products, arithmetic and copies ran while one was open for 6% of the time, Pallas kernels for 0%

commit v1 on v0

v1 whole, which is shorter than its diff:
```python
import functools
import math

import jax
import jax.numpy as jnp
from jax import lax
from jax.experimental import pallas as pl
from jax.experimental.pallas import tpu as pltpu
from jax.sharding import PartitionSpec as P

MESH = pl.DeviceIdType.MESH
BF, F32 = jnp.bfloat16, jnp.float32

N = 4
TOK = 48
HALF = 1536
SUB = HALF // 2
FEAT = 2 * HALF
HID = 768
BLOCK = 384
CHUNK = 96
GTILE = 512


def gelu_slope(pre):
    coeff = math.sqrt(2.0 / math.pi)
    inner = coeff * (pre + 0.044715 * pre * pre * pre)
    tanh_val = jnp.tanh(inner)
    return 0.5 * (1.0 + tanh_val) + 0.5 * pre * (1.0 - tanh_val * tanh_val) * coeff * (
        1.0 + 3.0 * 0.044715 * pre * pre
    )


class Slots:
    def __init__(self, ref, size):
        self.ref, self.size, self.keys = ref, size, {}

    def __getitem__(self, key):
        place = self.keys.setdefault(key, len(self.keys))
        assert place < self.size
        return self.ref.at[place]


AG_SEMS, SIB_SEMS, G_SEMS, PS_SEMS, RS_SEMS, LOCAL_SEMS = 44, 32, 12, 16, 44, 16


def kernel(
    x_hbm, w_hbm, pre_hbm, gh_hbm, gi_ref, gw_hbm,
    xall, gall, pre, gh, w, part, psib, r1, r2, r3, r4, gwb,
    ag_s, ag_r, sib_s, sib_r, g_s, g_r, ps_s, ps_r, rs_s, rs_r, local,
):
    dep, row, x = lax.axis_index("depth"), lax.axis_index("row"), lax.axis_index("col")
    z_lo, core = dep // 2, dep % 2
    y, z = row // 2, (row % 2) * 2 + z_lo
    place = {"x": x, "y": y, "z": z}

    def device(x, y, z, core):
        return ((z % 2) * 2 + core, y * 2 + z // 2, x)

    def towards(axis, step):
        there = dict(place)
        there[axis] = (place[axis] + step) % N
        return device(there["x"], there["y"], there["z"], core)

    sibling = device(x, y, z, 1 - core)

    ag_s, ag_r = Slots(ag_s, 64), Slots(ag_r, AG_SEMS)
    sib_s, sib_r = Slots(sib_s, SIB_SEMS), Slots(sib_r, SIB_SEMS)
    g_s, g_r = Slots(g_s, G_SEMS), Slots(g_r, G_SEMS)
    ps_s, ps_r = Slots(ps_s, PS_SEMS), Slots(ps_r, PS_SEMS)
    rs_s, rs_r = Slots(rs_s, RS_SEMS), Slots(rs_r, RS_SEMS)
    local = Slots(local, LOCAL_SEMS)

    barrier = pltpu.get_barrier_semaphore()
    neighbours = [sibling] + [towards(axis, step) for axis in "xyz" for step in (1, -1)]
    for there in neighbours:
        pl.semaphore_signal(barrier, inc=1, device_id=there, device_id_type=MESH)

    own_row = pl.multiple_of((dep * 8 + row) * TOK, 16)
    loads = {
        "pre": pltpu.make_async_copy(pre_hbm, pre, local["pre"]),
        "gh": pltpu.make_async_copy(gh_hbm, gh, local["gh"]),
        "x0": pltpu.make_async_copy(x_hbm.at[:, pl.ds(0, HALF)], xall.at[0, pl.ds(own_row, TOK)], local["x0"]),
        "x1": pltpu.make_async_copy(x_hbm.at[:, pl.ds(HALF, HALF)], xall.at[1, pl.ds(own_row, TOK)], local["x1"]),
        "w": pltpu.make_async_copy(w_hbm, w, local["w"]),
    }
    for name in ("x0", "x1", "pre", "gh", "w"):
        loads[name].start()

    pending = []

    def send(src, dst, s, r, there):
        copy = pltpu.make_async_remote_copy(
            src_ref=src, dst_ref=dst, send_sem=s, recv_sem=r, device_id=there, device_id_type=MESH
        )
        copy.start()
        return copy

    def arrived(dst, s, r):
        pltpu.make_async_remote_copy(
            src_ref=dst, dst_ref=dst, send_sem=s, recv_sem=r, device_id=sibling, device_id_type=MESH
        ).wait_recv()

    def drain():
        while pending:
            pending.pop(0).wait_send()

    axes = (("y", "z"), ("z", "y"))

    def x_rows(h, o1, o2, of_core):
        first, second = (place[axes[h][0]] + o1) % N, (place[axes[h][1]] + o2) % N
        yy, zz = (first, second) if h == 0 else (second, first)
        return pl.multiple_of((((zz % 2) * 2 + of_core) * 8 + yy * 2 + zz // 2) * TOK, 16)

    def x_block(h, o1, o2, sub, of_core):
        rows = pl.ds(x_rows(h, o1, o2, of_core), TOK)
        if sub is None:
            return xall.at[h, rows]
        return xall.at[h, rows, pl.ds(sub * SUB, SUB)]

    def x_send(h, o1, o2, sub, along, step):
        block = x_block(h, o1, o2, sub, core)
        there = ((o1 - step) % N, o2) if along == 0 else (o1, (o2 - step) % N)
        pending.append(
            send(block, block, ag_s[h, o1, o2, sub, along, step], ag_r[(h, *there, sub)], towards(axes[h][along], step))
        )

    def x_arrived(h, o1, o2, sub):
        arrived(x_block(h, o1, o2, sub, core), ag_s[h, 0, 0, None, 0, 1], ag_r[h, o1, o2, sub])

    def x_share(h, o1, o2):
        block = x_block(h, o1, o2, None, core)
        pending.append(send(block, block, sib_s[h, o1, o2], sib_r[h, o1, o2], sibling))

    def x_shared(h, o1, o2):
        arrived(x_block(h, o1, o2, None, 1 - core), sib_s[h, 0, 0], sib_r[h, o1, o2])

    def x_first(h, o1):
        x_arrived(h, o1, 0, None)
        x_send(h, o1, 0, 0 if o1 == 3 else 1, 0, 1 if o1 == 3 else -1)
        x_send(h, o1, 0, None, 1, 1)
        x_send(h, o1, 0, None, 1, -1)
        x_share(h, o1, 0)

    def x_far(h):
        for sub in (0, 1):
            x_arrived(h, 2, 0, sub)
            x_send(h, 2, 0, sub, 1, 1)
            x_send(h, 2, 0, sub, 1, -1)
        x_share(h, 2, 0)

    def x_second(h, o1):
        if o1 == 2:
            for o2, sub in ((3, 0), (1, 1)):
                x_arrived(h, 2, o2, sub)
                x_send(h, 2, o2, sub, 1, 1 if o2 == 3 else -1)
            for o2, sub in ((3, 1), (1, 0)):
                x_arrived(h, 2, o2, sub)
                x_share(h, 2, o2)
            return
        for o2 in (3, 1):
            x_arrived(h, o1, o2, None)
            x_send(h, o1, o2, 0 if o2 == 3 else 1, 1, 1 if o2 == 3 else -1)
            x_share(h, o1, o2)

    def x_last(h, o1):
        for sub in (0, 1):
            x_arrived(h, o1, 2, sub)
        x_share(h, o1, 2)

    def g_block(o, q):
        return gall.at[pl.ds(pl.multiple_of(((x + o) % N) * BLOCK + q * CHUNK, 16), CHUNK)]

    def g_send(o, q, step):
        block = g_block(o, q)
        pending.append(send(block, block, g_s[o, q, step], g_r[(o - step) % N, q], towards("x", step)))

    def g_arrived(o, q):
        arrived(g_block(o, q), g_s[0, 0, 1], g_r[o, q])

    def g_forward(o, q):
        g_arrived(o, q)
        g_send(o, q, 1 if o == 3 else -1)

    def g_compute(q):
        @pl.loop(0, CHUNK // 32)
        def _(i):
            rows = pl.ds(pl.multiple_of(q * CHUNK + i * 32, 32), 32)
            slope = gelu_slope(pre[rows].astype(F32))
            value = (gh[rows].astype(F32) * slope).astype(BF)
            gall[pl.ds(pl.multiple_of(x * BLOCK + q * CHUNK + i * 32, 32), 32)] = value

    def partial(o):
        block = (x + o) % N
        away, z_of = (block + core) % 2, block // 2
        rows = pl.ds(pl.multiple_of(block * BLOCK, 16), BLOCK)
        for h in (0, 1):
            @pl.loop(0, 2)
            def _(n):
                product = lax.dot_general(
                    gall[rows],
                    w[pl.ds(pl.multiple_of(h * HALF + n * SUB, SUB), SUB)],
                    (((1,), (1,)), ((), ())),
                    preferred_element_type=F32,
                )
                part[away, z_of, h, :, pl.ds(pl.multiple_of(n * SUB, SUB), SUB)] = product.astype(BF)

            @pl.when(away == 1)
            def _():
                for yy in range(N):
                    piece = pl.ds(yy * CHUNK, CHUNK)
                    slot = (o // 2 * 2 + h) * N + yy
                    send(
                        part.at[1, z_of, h, piece], psib.at[z_of, h, piece],
                        ps_s.ref.at[slot], ps_r.ref.at[(z_of * 2 + h) * N + yy], sibling,
                    )

    def sib_part(zl, h, yy):
        piece = psib.at[zl, h, pl.ds(pl.multiple_of(yy * CHUNK, 16), CHUNK)]
        arrived(piece, ps_s.ref.at[0], ps_r.ref.at[(zl * 2 + h) * N + yy])

    rs_axes = (("z", "y"), ("y", "z"))

    def target(h, oa, ob):
        a, b = (place[rs_axes[h][0]] + oa) % N, (place[rs_axes[h][1]] + ob) % N
        zz, yy = (a, b) if h == 0 else (b, a)
        return zz % 2, pl.multiple_of(yy * CHUNK + (zz // 2) * TOK, 16), yy

    def rows16(body):
        @pl.loop(0, TOK // 16)
        def _(i):
            body(pl.multiple_of(i * 16, 16))

    def whole(h, zl, row0, i):
        at = pl.ds(pl.multiple_of(row0 + i, 16), 16)
        return part[0, zl, h, at].astype(F32) + psib[zl, h, at].astype(F32)

    def first_step(h, ob):
        zl, row0, yy = target(h, 2, ob)
        if h == 0 or ob in (2, 1):
            sib_part(zl, h, yy)

        def add(i):
            part[0, zl, h, pl.ds(pl.multiple_of(row0 + i, 16), 16)] = whole(h, zl, row0, i).astype(BF)

        rows16(add)
        for sub, step in ((0, 1), (1, -1)):
            pending.append(send(
                part.at[0, zl, h, pl.ds(row0, TOK), pl.ds(sub * SUB, SUB)], r1.at[h, sub, ob],
                rs_s[1, h, sub, ob], rs_r[1, h, sub, ob], towards(rs_axes[h][0], step),
            ))

    def second_step(h, ob):
        for sub, oa, step in ((0, 1, 1), (1, 3, -1)):
            zl, row0, yy = target(h, oa, ob)
            if (h == 0 and sub == 0) or (h == 1 and ob in (2, 1)):
                sib_part(zl, h, yy)
            arrived(r1.at[h, sub, ob], rs_s[1, h, sub, ob], rs_r[1, h, sub, ob])
            got, kept = pl.ds(sub * SUB, SUB), pl.ds((1 - sub) * SUB, SUB)

            def add(i):
                at = pl.ds(pl.multiple_of(row0 + i, 16), 16)
                part[0, zl, h, at, got] = (
                    part[0, zl, h, at, got].astype(F32) + psib[zl, h, at, got].astype(F32)
                    + r1[h, sub, ob, pl.ds(i, 16)].astype(F32)
                ).astype(BF)
                part[0, zl, h, at, kept] = (
                    part[0, zl, h, at, kept].astype(F32) + psib[zl, h, at, kept].astype(F32)
                ).astype(BF)

            rows16(add)
            pending.append(send(
                part.at[0, zl, h, pl.ds(row0, TOK)], r2.at[h, sub, ob],
                rs_s[2, h, sub, ob], rs_r[2, h, sub, ob], towards(rs_axes[h][0], step),
            ))

    def third_step(h, ob):
        zl, row0, yy = target(h, 0, ob)
        if h == 1 and ob in (2, 1):
            sib_part(zl, h, yy)
        for sub in (0, 1):
            arrived(r2.at[h, sub, ob], rs_s[2, h, sub, ob], rs_r[2, h, sub, ob])

        def add(i):
            at = pl.ds(i, 16)
            part[0, zl, h, pl.ds(pl.multiple_of(row0 + i, 16), 16)] = (
                whole(h, zl, row0, i) + r2[h, 0, ob, at].astype(F32) + r2[h, 1, ob, at].astype(F32)
            ).astype(BF)

        rows16(add)

    def fourth_step(h):
        zl, row0, _ = target(h, 0, 2)
        for sub, step in ((0, 1), (1, -1)):
            pending.append(send(
                part.at[0, zl, h, pl.ds(row0, TOK), pl.ds(sub * SUB, SUB)], r3.at[h, sub],
                rs_s[3, h, sub], rs_r[3, h, sub], towards(rs_axes[h][1], step),
            ))

    def fifth_step_early(h):
        for sub, ob, step in ((0, 1, 1), (1, 3, -1)):
            zl, row0, _ = target(h, 0, ob)
            kept = pl.ds((1 - sub) * SUB, SUB)
            pending.append(send(
                part.at[0, zl, h, pl.ds(row0, TOK), kept], r4.at[h, sub, :, kept],
                rs_s[4, h, sub, 1], rs_r[4, h, sub, 1], towards(rs_axes[h][1], step),
            ))

    def fifth_step(h):
        for sub, ob, step in ((0, 1, 1), (1, 3, -1)):
            zl, row0, _ = target(h, 0, ob)
            got = pl.ds(sub * SUB, SUB)
            arrived(r3.at[h, sub], rs_s[3, h, sub], rs_r[3, h, sub])

            def add(i):
                at = pl.ds(pl.multiple_of(row0 + i, 16), 16)
                part[0, zl, h, at, got] = (
                    part[0, zl, h, at, got].astype(F32) + r3[h, sub, pl.ds(i, 16)].astype(F32)
                ).astype(BF)

            rows16(add)
            pending.append(send(
                part.at[0, zl, h, pl.ds(row0, TOK), got], r4.at[h, sub, :, got],
                rs_s[4, h, sub, 0], rs_r[4, h, sub, 0], towards(rs_axes[h][1], step),
            ))

    def sixth_step(h):
        zl, row0, _ = target(h, 0, 0)
        for sub in (0, 1):
            for late in (1, 0):
                cols = pl.ds((sub if late == 0 else 1 - sub) * SUB, SUB)
                arrived(r4.at[h, sub, :, cols], rs_s[4, h, sub, late], rs_r[4, h, sub, late])

        def add(i):
            at = pl.ds(i, 16)
            gi_ref[at, pl.ds(h * HALF, HALF)] = (
                part[0, zl, h, pl.ds(pl.multiple_of(row0 + i, 16), 16)].astype(F32)
                + r4[h, 0, at].astype(F32) + r4[h, 1, at].astype(F32)
            ).astype(BF)

        rows16(add)

    tiles = HALF // GTILE
    stores = []

    def weight_tile(n):
        h, m = n // tiles, n % tiles
        product = lax.dot_general(
            xall[h, :, pl.ds(m * GTILE, GTILE)], gall[...], (((0,), (0,)), ((), ())), preferred_element_type=F32
        )
        rows = pl.ds(n * GTILE, GTILE)
        gwb[rows] = product.astype(BF)
        store = pltpu.make_async_copy(gwb.at[rows], gw_hbm.at[rows], local["gw", n])
        store.start()
        stores.append(store)

    loads["x0"].wait()
    loads["x1"].wait()
    loads["pre"].wait()
    loads["gh"].wait()
    g_compute(0)
    pl.semaphore_wait(barrier, len(neighbours))
    for along in (0, 1):
        for h in (0, 1):
            for step in (1, -1):
                x_send(h, 0, 0, None, along, step)
    for h in (0, 1):
        x_share(h, 0, 0)
    for q in (0, 2, 1, 3):
        if q:
            g_compute(q)
        g_send(0, q, 1)
        g_send(0, q, -1)
    loads["w"].wait()
    partial(0)
    for o in (3, 1):
        for h in (0, 1):
            x_first(h, o)
    g_forward(3, 0)
    g_forward(1, 2)
    for h in (0, 1):
        x_second(h, 0)
    for h in (0, 1):
        x_far(h)
    g_forward(3, 1)
    g_forward(1, 3)
    for h in (0, 1):
        x_second(h, 3)
    for h in (0, 1):
        x_second(h, 1)
    for h in (0, 1):
        x_last(h, 0)
    for q in (2, 3):
        g_arrived(3, q)
    partial(3)
    for q in (0, 1):
        g_arrived(1, q)
    partial(1)
    for h in (0, 1):
        x_second(h, 2)
    for q in range(4):
        g_arrived(2, q)
    partial(2)
    order = (2, 1, 3, 0)
    for ob in order:
        for h in (0, 1):
            first_step(h, ob)
    for ob in order:
        for h in (0, 1):
            second_step(h, ob)
    for o1 in (3, 1, 2):
        for h in (0, 1):
            x_last(h, o1)
    for o1 in range(N):
        for o2 in range(N):
            for h in (0, 1):
                x_shared(h, o1, o2)
    for n in range(3):
        weight_tile(n)
    for h in (0, 1):
        third_step(h, 2)
        fourth_step(h)
    weight_tile(3)
    for ob in (1, 3):
        for h in (0, 1):
            third_step(h, ob)
    for h in (0, 1):
        fifth_step_early(h)
    weight_tile(4)
    weight_tile(5)
    for slot in range(PS_SEMS):
        piece = part.at[1, 0, 0, pl.ds(0, CHUNK)]
        pltpu.make_async_remote_copy(
            src_ref=piece, dst_ref=piece, send_sem=ps_s.ref.at[slot], recv_sem=ps_r.ref.at[0],
            device_id=sibling, device_id_type=MESH,
        ).wait_send()
    for h in (0, 1):
        third_step(h, 0)
    for h in (0, 1):
        fifth_step(h)
    drain()
    for store in stores:
        store.wait()
    for h in (0, 1):
        sixth_step(h)


def per_device(inputs, weight, pre_act, grad_hidden):
    dma = pltpu.SemaphoreType.DMA
    return pl.pallas_call(
        kernel,
        out_shape=(
            jax.ShapeDtypeStruct((TOK, FEAT), BF),
            jax.ShapeDtypeStruct((FEAT, HID), BF),
        ),
        in_specs=[pl.BlockSpec(memory_space=pl.ANY)] * 4,
        out_specs=(pl.BlockSpec(memory_space=pltpu.VMEM), pl.BlockSpec(memory_space=pl.ANY)),
        scratch_shapes=[
            pltpu.VMEM((2, N * BLOCK, HALF), BF),
            pltpu.VMEM((N * BLOCK, HID), BF),
            pltpu.VMEM((BLOCK, HID), BF),
            pltpu.VMEM((BLOCK, HID), BF),
            pltpu.VMEM((FEAT, HID), BF),
            pltpu.VMEM((2, 2, 2, BLOCK, HALF), BF),
            pltpu.VMEM((2, 2, BLOCK, HALF), BF),
            pltpu.VMEM((2, 2, N, TOK, SUB), BF),
            pltpu.VMEM((2, 2, N, TOK, HALF), BF),
            pltpu.VMEM((2, 2, TOK, SUB), BF),
            pltpu.VMEM((2, 2, TOK, HALF), BF),
            pltpu.VMEM((FEAT, HID), BF),
            dma((64,)), dma((AG_SEMS,)),
            dma((SIB_SEMS,)), dma((SIB_SEMS,)),
            dma((G_SEMS,)), dma((G_SEMS,)),
            dma((PS_SEMS,)), dma((PS_SEMS,)),
            dma((RS_SEMS,)), dma((RS_SEMS,)),
            dma((LOCAL_SEMS,)),
        ],
        compiler_params=pltpu.CompilerParams(
            collective_id=0, has_side_effects=True, vmem_limit_bytes=58 << 20
        ),
        cost_estimate=pl.CostEstimate(flops=14_500_000_000, bytes_accessed=16_000_000, transcendentals=300_000),
        name="gelu_up_backward",
    )(inputs, weight, pre_act, grad_hidden)


def solution(mesh):
    return jax.shard_map(
        per_device,
        mesh=mesh,
        in_specs=(
            P(("depth", "row"), "col"),
            P("col", ("depth", "row")),
            P("col", ("depth", "row")),
            P("col", ("depth", "row")),
        ),
        out_specs=(P(("depth", "row"), "col"), P("col", ("depth", "row"))),
        check_vma=False,
    )
```

time: 560 us -> 72.4 us (0.13)
  waiting for transfers between devices: 507 us -> 0 us
  Pallas kernels: 0 us -> 64.3 us
  matrix products: 26.7 us -> 0 us
  between operations: 13.7 us -> 0.64 us
    reduce_scatter x1 -> x0, waiting for transfers between devices: 389 us -> none  [per_device(): lax.psum_scatter(lax.dot_general(rows, weight, (((1,), (1,)), ((), ())),...]
    all_gather x2 -> x0, waiting for transfers between devices: 118 us -> none  [the longest x1 82 us: per_device(): lax.all_gather(inputs, ('depth', 'row'), axis=0, tiled=True)]
    pallas_call x0 -> x1, Pallas kernels: none -> 64.3 us  [per_device(): pl.pallas_call(kernel, out_shape=(jax.ShapeDtypeStruct((TOK, FEAT), BF),...]
    dot_general x2 -> x0, matrix products: 26.7 us -> none  [the longest x1 13.8 us: per_device(): lax.dot_general(rows, weight, (((1,), (1,)), ((), ())), preferred_element...]
  transfers between devices with their start and end apart: 3 -> 0, of which waited for: 3 -> 0; matrix products, arithmetic and copies ran while one was open for 6% -> 0% of each run, Pallas kernels for 0% -> 0%
where the time goes in v1:
time: 72.4 us; the launch traced here: 71.5 us
  Pallas kernels  64.3 us (89%)
  local copies, waits for them, and re-layouts  6.52 us (9%)
    pallas_call x1, Pallas kernels, per_device(): pl.pallas_call(kernel, out_shape=(jax.ShapeDtypeStruct((TOK, FEAT), BF),...  64.3 us
    unnamed x2, local copies, waits for them, and re-layouts  6.52 us

profile of v1, /device:TPU:1, one launch (start us, length us, event | category | flops | bytes accessed | tf_op | source)
XLA Modules:
  0.0 71.5 jit_solution(3067428016220231280)
XLA Ops:
  0.6 64.3 %gelu_up_backward.1 = (bf16[48,3072]{1,0:T(8,128)(2,1)}, bf16[3072,768]{1,0:T(8,128)(2,1)}) custom-call(bf16[48,3072]{1,0:T(8,128)(2,1)} %x_hbm.1, bf16[3072,768]{1,0:T(8,128)(2,1)} %w_hbm.1, bf16[384,768]{1,0:T(8,128)(2,1)} %pre_hbm.1, bf16[384,768]{1,0:T(8,128)(2,1)} %gh_hbm.1), custom_call_target="tpu_custom_call" | custom-call | flops 14499999744 | bytes 16000000 | tf_op jit(solution)/shard_map/gelu_up_backward/pallas_call | solution.py:450
  64.9 1.7 %copy.8 = bf16[48,3072]{1,0:T(8,128)(2,1)} copy(bf16[48,3072]{1,0:T(8,128)(2,1)} %get-tuple-element.4) | data formatting | bytes 589824
  66.6 4.8 %copy.9 = bf16[3072,768]{1,0:T(8,128)(2,1)} copy(bf16[3072,768]{1,0:T(8,128)(2,1)} %get-tuple-element.5) | data formatting | bytes 9437184

commit v2 on v1

--- a/solution.py
+++ b/solution.py
@@ -20,6 +20,7 @@
 BLOCK = 384
 CHUNK = 96
 GTILE = 512
+WRITES = 4
 
 
 def gelu_slope(pre):
@@ -45,8 +46,8 @@
 
 
 def kernel(
-    x_hbm, w_hbm, pre_hbm, gh_hbm, gi_ref, gw_hbm,
-    xall, gall, pre, gh, w, part, psib, r1, r2, r3, r4, gwb,
+    x_hbm, w_hbm, pre_hbm, gh_hbm, gi_ref, gwb,
+    xall, gall, pre, gh, w, part, psib, r1, r2, r3, r4, own, onward,
     ag_s, ag_r, sib_s, sib_r, g_s, g_r, ps_s, ps_r, rs_s, rs_r, local,
 ):
     dep, row, x = lax.axis_index("depth"), lax.axis_index("row"), lax.axis_index("col")
@@ -138,8 +139,10 @@
     def x_first(h, o1):
         x_arrived(h, o1, 0, None)
         x_send(h, o1, 0, 0 if o1 == 3 else 1, 0, 1 if o1 == 3 else -1)
-        x_send(h, o1, 0, None, 1, 1)
-        x_send(h, o1, 0, None, 1, -1)
+
+    def x_turn(h, o1):
+        for step in (1, -1):
+            x_send(h, o1, 0, None, 1, step)
         x_share(h, o1, 0)
 
     def x_far(h):
@@ -190,30 +193,29 @@
             value = (gh[rows].astype(F32) * slope).astype(BF)
             gall[pl.ds(pl.multiple_of(x * BLOCK + q * CHUNK + i * 32, 32), 32)] = value
 
-    def partial(o):
+    def partial(o, h):
         block = (x + o) % N
         away, z_of = (block + core) % 2, block // 2
         rows = pl.ds(pl.multiple_of(block * BLOCK, 16), BLOCK)
-        for h in (0, 1):
-            @pl.loop(0, 2)
-            def _(n):
-                product = lax.dot_general(
-                    gall[rows],
-                    w[pl.ds(pl.multiple_of(h * HALF + n * SUB, SUB), SUB)],
-                    (((1,), (1,)), ((), ())),
-                    preferred_element_type=F32,
+        @pl.loop(0, 2)
+        def _(n):
+            product = lax.dot_general(
+                gall[rows],
+                w[pl.ds(pl.multiple_of(h * HALF + n * SUB, SUB), SUB)],
+                (((1,), (1,)), ((), ())),
+                preferred_element_type=F32,
+            )
+            part[away, z_of, h, :, pl.ds(pl.multiple_of(n * SUB, SUB), SUB)] = product.astype(BF)
+
+        @pl.when(away == 1)
+        def _():
+            for yy in range(N):
+                piece = pl.ds(yy * CHUNK, CHUNK)
+                slot = (o // 2 * 2 + h) * N + yy
+                send(
+                    part.at[1, z_of, h, piece], psib.at[z_of, h, piece],
+                    ps_s.ref.at[slot], ps_r.ref.at[(z_of * 2 + h) * N + yy], sibling,
                 )
-                part[away, z_of, h, :, pl.ds(pl.multiple_of(n * SUB, SUB), SUB)] = product.astype(BF)
-
-            @pl.when(away == 1)
-            def _():
-                for yy in range(N):
-                    piece = pl.ds(yy * CHUNK, CHUNK)
-                    slot = (o // 2 * 2 + h) * N + yy
-                    send(
-                        part.at[1, z_of, h, piece], psib.at[z_of, h, piece],
-                        ps_s.ref.at[slot], ps_r.ref.at[(z_of * 2 + h) * N + yy], sibling,
-                    )
 
     def sib_part(zl, h, yy):
         piece = psib.at[zl, h, pl.ds(pl.multiple_of(yy * CHUNK, 16), CHUNK)]
@@ -282,10 +284,18 @@
             arrived(r2.at[h, sub, ob], rs_s[2, h, sub, ob], rs_r[2, h, sub, ob])
 
         def add(i):
-            at = pl.ds(i, 16)
-            part[0, zl, h, pl.ds(pl.multiple_of(row0 + i, 16), 16)] = (
-                whole(h, zl, row0, i) + r2[h, 0, ob, at].astype(F32) + r2[h, 1, ob, at].astype(F32)
-            ).astype(BF)
+            at, here = pl.ds(i, 16), pl.ds(pl.multiple_of(row0 + i, 16), 16)
+            total = whole(h, zl, row0, i) + r2[h, 0, ob, at].astype(F32) + r2[h, 1, ob, at].astype(F32)
+            if ob == 0:
+                own[h, at] = total
+            elif ob == 2:
+                part[0, zl, h, here] = total.astype(BF)
+            else:
+                sub = 0 if ob == 1 else 1
+                onward[h, sub, at] = total[:, sub * SUB:(sub + 1) * SUB]
+                part[0, zl, h, here, pl.ds((1 - sub) * SUB, SUB)] = (
+                    total[:, (1 - sub) * SUB:(2 - sub) * SUB].astype(BF)
+                )
 
         rows16(add)
 
@@ -297,35 +307,34 @@
                 rs_s[3, h, sub], rs_r[3, h, sub], towards(rs_axes[h][1], step),
             ))
 
-    def fifth_step_early(h):
-        for sub, ob, step in ((0, 1, 1), (1, 3, -1)):
-            zl, row0, _ = target(h, 0, ob)
-            kept = pl.ds((1 - sub) * SUB, SUB)
-            pending.append(send(
-                part.at[0, zl, h, pl.ds(row0, TOK), kept], r4.at[h, sub, :, kept],
-                rs_s[4, h, sub, 1], rs_r[4, h, sub, 1], towards(rs_axes[h][1], step),
-            ))
-
-    def fifth_step(h):
-        for sub, ob, step in ((0, 1, 1), (1, 3, -1)):
-            zl, row0, _ = target(h, 0, ob)
-            got = pl.ds(sub * SUB, SUB)
-            arrived(r3.at[h, sub], rs_s[3, h, sub], rs_r[3, h, sub])
-
-            def add(i):
-                at = pl.ds(pl.multiple_of(row0 + i, 16), 16)
-                part[0, zl, h, at, got] = (
-                    part[0, zl, h, at, got].astype(F32) + r3[h, sub, pl.ds(i, 16)].astype(F32)
-                ).astype(BF)
-
-            rows16(add)
-            pending.append(send(
-                part.at[0, zl, h, pl.ds(row0, TOK), got], r4.at[h, sub, :, got],
-                rs_s[4, h, sub, 0], rs_r[4, h, sub, 0], towards(rs_axes[h][1], step),
-            ))
+    def fifth_step_early(h, sub):
+        ob, step = ((1, 1), (3, -1))[sub]
+        zl, row0, _ = target(h, 0, ob)
+        kept = pl.ds((1 - sub) * SUB, SUB)
+        pending.append(send(
+            part.at[0, zl, h, pl.ds(row0, TOK), kept], r4.at[h, sub, :, kept],
+            rs_s[4, h, sub, 1], rs_r[4, h, sub, 1], towards(rs_axes[h][1], step),
+        ))
+
+    def fifth_step(h, sub):
+        ob, step = ((1, 1), (3, -1))[sub]
+        zl, row0, _ = target(h, 0, ob)
+        got = pl.ds(sub * SUB, SUB)
+        arrived(r3.at[h, sub], rs_s[3, h, sub], rs_r[3, h, sub])
+
+        def add(i):
+            at = pl.ds(i, 16)
+            part[0, zl, h, pl.ds(pl.multiple_of(row0 + i, 16), 16), got] = (
+                onward[h, sub, at] + r3[h, sub, at].astype(F32)
+            ).astype(BF)
+
+        rows16(add)
+        pending.append(send(
+            part.at[0, zl, h, pl.ds(row0, TOK), got], r4.at[h, sub, :, got],
+            rs_s[4, h, sub, 0], rs_r[4, h, sub, 0], towards(rs_axes[h][1], step),
+        ))
 
     def sixth_step(h):
-        zl, row0, _ = target(h, 0, 0)
         for sub in (0, 1):
             for late in (1, 0):
                 cols = pl.ds((sub if late == 0 else 1 - sub) * SUB, SUB)
@@ -334,14 +343,12 @@
         def add(i):
             at = pl.ds(i, 16)
             gi_ref[at, pl.ds(h * HALF, HALF)] = (
-                part[0, zl, h, pl.ds(pl.multiple_of(row0 + i, 16), 16)].astype(F32)
-                + r4[h, 0, at].astype(F32) + r4[h, 1, at].astype(F32)
+                own[h, at] + r4[h, 0, at].astype(F32) + r4[h, 1, at].astype(F32)
             ).astype(BF)
 
         rows16(add)
 
     tiles = HALF // GTILE
-    stores = []
 
     def weight_tile(n):
         h, m = n // tiles, n % tiles
@@ -350,83 +357,90 @@
         )
         rows = pl.ds(n * GTILE, GTILE)
         gwb[rows] = product.astype(BF)
-        store = pltpu.make_async_copy(gwb.at[rows], gw_hbm.at[rows], local["gw", n])
-        store.start()
-        stores.append(store)
-
+
+    both = (0, 1)
+    loads["pre"].wait()
+    loads["gh"].wait()
+    for q in range(4):
+        g_compute(q)
     loads["x0"].wait()
     loads["x1"].wait()
-    loads["pre"].wait()
-    loads["gh"].wait()
-    g_compute(0)
     pl.semaphore_wait(barrier, len(neighbours))
     for along in (0, 1):
-        for h in (0, 1):
+        for h in both:
             for step in (1, -1):
                 x_send(h, 0, 0, None, along, step)
-    for h in (0, 1):
-        x_share(h, 0, 0)
     for q in (0, 2, 1, 3):
-        if q:
-            g_compute(q)
         g_send(0, q, 1)
         g_send(0, q, -1)
+    for h in both:
+        x_share(h, 0, 0)
     loads["w"].wait()
-    partial(0)
+    for h in both:
+        partial(0, h)
     for o in (3, 1):
-        for h in (0, 1):
+        for h in both:
             x_first(h, o)
+    for o in (3, 1):
+        for h in both:
+            x_turn(h, o)
     g_forward(3, 0)
     g_forward(1, 2)
-    for h in (0, 1):
+    for h in both:
         x_second(h, 0)
-    for h in (0, 1):
-        x_far(h)
     g_forward(3, 1)
     g_forward(1, 3)
-    for h in (0, 1):
+    for h in both:
+        x_far(h)
+    for h in both:
         x_second(h, 3)
-    for h in (0, 1):
-        x_second(h, 1)
-    for h in (0, 1):
-        x_last(h, 0)
     for q in (2, 3):
         g_arrived(3, q)
-    partial(3)
+    partial(3, 0)
+    for h in both:
+        x_second(h, 1)
+    partial(3, 1)
     for q in (0, 1):
         g_arrived(1, q)
-    partial(1)
-    for h in (0, 1):
+    partial(1, 0)
+    for h in both:
+        x_last(h, 0)
+    partial(1, 1)
+    for h in both:
         x_second(h, 2)
     for q in range(4):
         g_arrived(2, q)
-    partial(2)
-    order = (2, 1, 3, 0)
-    for ob in order:
-        for h in (0, 1):
+    for h in both:
+        partial(2, h)
+    for h in both:
+        for ob in (2, 1, 3, 0):
             first_step(h, ob)
-    for ob in order:
-        for h in (0, 1):
+    for ob in (2, 1, 3):
+        for h in both:
             second_step(h, ob)
     for o1 in (3, 1, 2):
-        for h in (0, 1):
+        for h in both:
             x_last(h, o1)
     for o1 in range(N):
         for o2 in range(N):
-            for h in (0, 1):
+            for h in both:
                 x_shared(h, o1, o2)
-    for n in range(3):
-        weight_tile(n)
-    for h in (0, 1):
+    weight_tile(0)
+    weight_tile(1)
+    for h in both:
         third_step(h, 2)
         fourth_step(h)
+    for h in both:
+        second_step(h, 0)
+    weight_tile(2)
     weight_tile(3)
-    for ob in (1, 3):
-        for h in (0, 1):
-            third_step(h, ob)
-    for h in (0, 1):
-        fifth_step_early(h)
+    for h in both:
+        third_step(h, 1)
+        fifth_step_early(h, 0)
     weight_tile(4)
+    for h in both:
+        third_step(h, 3)
+        fifth_step_early(h, 1)
     weight_tile(5)
     for slot in range(PS_SEMS):
         piece = part.at[1, 0, 0, pl.ds(0, CHUNK)]
@@ -434,27 +448,37 @@
             src_ref=piece, dst_ref=piece, send_sem=ps_s.ref.at[slot], recv_sem=ps_r.ref.at[0],
             device_id=sibling, device_id_type=MESH,
         ).wait_send()
-    for h in (0, 1):
+    for h in both:
+        for sub in (0, 1):
+            fifth_step(h, sub)
+    while len(pending) > 32:
+        pending.pop(0).wait_send()
+    for h in both:
         third_step(h, 0)
-    for h in (0, 1):
-        fifth_step(h)
+    for h in both:
+        sixth_step(h)
     drain()
-    for store in stores:
-        store.wait()
-    for h in (0, 1):
-        sixth_step(h)
+
+
+def write_out(gi, gw, gi_hbm, gw_hbm, sems):
+    rows = FEAT // WRITES
+    copies = [pltpu.make_async_copy(gi, gi_hbm, sems.at[WRITES])]
+    for n in range(WRITES):
+        part = pl.ds(n * rows, rows)
+        copies.append(pltpu.make_async_copy(gw.at[part], gw_hbm.at[part], sems.at[n]))
+    for copy in copies:
+        copy.start()
+    for copy in copies:
+        copy.wait()
 
 
 def per_device(inputs, weight, pre_act, grad_hidden):
     dma = pltpu.SemaphoreType.DMA
-    return pl.pallas_call(
+    grads = pl.pallas_call(
         kernel,
-        out_shape=(
-            jax.ShapeDtypeStruct((TOK, FEAT), BF),
-            jax.ShapeDtypeStruct((FEAT, HID), BF),
-        ),
+        out_shape=(pltpu.VMEM((TOK, FEAT), BF), pltpu.VMEM((FEAT, HID), BF)),
         in_specs=[pl.BlockSpec(memory_space=pl.ANY)] * 4,
-        out_specs=(pl.BlockSpec(memory_space=pltpu.VMEM), pl.BlockSpec(memory_space=pl.ANY)),
+        out_specs=(pl.BlockSpec(memory_space=pltpu.VMEM), pl.BlockSpec(memory_space=pltpu.VMEM)),
         scratch_shapes=[
             pltpu.VMEM((2, N * BLOCK, HALF), BF),
             pltpu.VMEM((N * BLOCK, HID), BF),
@@ -467,7 +491,8 @@
             pltpu.VMEM((2, 2, N, TOK, HALF), BF),
             pltpu.VMEM((2, 2, TOK, SUB), BF),
             pltpu.VMEM((2, 2, TOK, HALF), BF),
-            pltpu.VMEM((FEAT, HID), BF),
+            pltpu.VMEM((2, TOK, HALF), F32),
+            pltpu.VMEM((2, 2, TOK, SUB), F32),
             dma((64,)), dma((AG_SEMS,)),
             dma((SIB_SEMS,)), dma((SIB_SEMS,)),
             dma((G_SEMS,)), dma((G_SEMS,)),
@@ -476,11 +501,20 @@
             dma((LOCAL_SEMS,)),
         ],
         compiler_params=pltpu.CompilerParams(
-            collective_id=0, has_side_effects=True, vmem_limit_bytes=58 << 20
+            collective_id=0, has_side_effects=True, vmem_limit_bytes=50 << 20
         ),
         cost_estimate=pl.CostEstimate(flops=14_500_000_000, bytes_accessed=16_000_000, transcendentals=300_000),
         name="gelu_up_backward",
     )(inputs, weight, pre_act, grad_hidden)
+    return pl.pallas_call(
+        write_out,
+        out_shape=tuple(jax.ShapeDtypeStruct(g.shape, g.dtype) for g in grads),
+        in_specs=[pl.BlockSpec(memory_space=pltpu.VMEM)] * 2,
+        out_specs=[pl.BlockSpec(memory_space=pl.ANY)] * 2,
+        scratch_shapes=[dma((1 + WRITES,))],
+        compiler_params=pltpu.CompilerParams(vmem_limit_bytes=1 << 20),
+        name="write_out",
+    )(*(pltpu.with_memory_space_constraint(g, pltpu.VMEM) for g in grads))
 
 
 def solution(mesh):

time: 72.4 us -> 65.4 us (0.903); the launches traced: 71.5 us -> 65.3 us
  local copies, waits for them, and re-layouts: 6.52 us -> 0 us
    unnamed x2 -> x0, local copies, waits for them, and re-layouts: 6.52 us -> none
    pallas_call x1 -> x2, Pallas kernels: 64.3 us -> 64.7 us  [the longest x1 62.4 us: per_device(): pl.pallas_call(kernel, out_shape=(pltpu.VMEM((TOK, FEAT), BF), pltpu.VMEM...]
where the time goes in v2:
time: 65.4 us; the launch traced here: 65.3 us
  Pallas kernels  64.7 us (99%)
    pallas_call x1, Pallas kernels, per_device(): pl.pallas_call(kernel, out_shape=(pltpu.VMEM((TOK, FEAT), BF), pltpu.VMEM...  62.4 us
    pallas_call x1, Pallas kernels, per_device(): pl.pallas_call(write_out, out_shape=tuple((jax.ShapeDtypeStruct(g.shape,...  2.32 us

profile of v2, /device:TPU:1, one launch (start us, length us, event | category | flops | bytes accessed | tf_op | source)
XLA Modules:
  0.0 65.3 jit_solution(12279912723498640091)
XLA Ops:
  0.6 62.4 %gelu_up_backward.1 = (bf16[48,3072]{1,0:T(8,128)(2,1)S(1)}, bf16[3072,768]{1,0:T(8,128)(2,1)S(1)}) custom-call(bf16[48,3072]{1,0:T(8,128)(2,1)} %x_hbm.1, bf16[3072,768]{1,0:T(8,128)(2,1)} %w_hbm.1, bf16[384,768]{1,0:T(8,128)(2,1)} %pre_hbm.1, bf16[384,768]{1,0:T(8,128)(2,1)} %gh_hbm.1), custom_call_target="tpu_custom_call" | custom-call | flops 14499999744 | bytes 16000000 | tf_op jit(solution)/shard_map/gelu_up_backward/pallas_call | solution.py:477
  63.0 2.3 %write_out.1 = (bf16[48,3072]{1,0:T(8,128)(2,1)}, bf16[3072,768]{1,0:T(8,128)(2,1)}) custom-call(bf16[48,3072]{1,0:T(8,128)(2,1)S(1)} %get-tuple-element.4.gi, bf16[3072,768]{1,0:T(8,128)(2,1)S(1)} %get-tuple-element.5.gw), custom_call_target="tpu_custom_call" | custom-call | tf_op jit(solution)/shard_map/write_out/pallas_call | solution.py:509

commit v3 on v2

--- a/solution.py
+++ b/solution.py
@@ -102,8 +102,8 @@
             src_ref=dst, dst_ref=dst, send_sem=s, recv_sem=r, device_id=sibling, device_id_type=MESH
         ).wait_recv()
 
-    def drain():
-        while pending:
+    def drain(left):
+        while len(pending) > left:
             pending.pop(0).wait_send()
 
     axes = (("y", "z"), ("z", "y"))
@@ -125,6 +125,13 @@
         pending.append(
             send(block, block, ag_s[h, o1, o2, sub, along, step], ag_r[(h, *there, sub)], towards(axes[h][along], step))
         )
+
+    def x_send_own(h, along, step):
+        there = (-step % N, 0) if along == 0 else (0, -step % N)
+        pending.append(send(
+            x_hbm.at[:, pl.ds(h * HALF, HALF)], x_block(h, 0, 0, None, core),
+            ag_s[h, 0, 0, None, along, step], ag_r[(h, *there, None)], towards(axes[h][along], step),
+        ))
 
     def x_arrived(h, o1, o2, sub):
         arrived(x_block(h, o1, o2, sub, core), ag_s[h, 0, 0, None, 0, 1], ag_r[h, o1, o2, sub])
@@ -247,9 +254,18 @@
 
         rows16(add)
         for sub, step in ((0, 1), (1, -1)):
-            pending.append(send(
+            send(
                 part.at[0, zl, h, pl.ds(row0, TOK), pl.ds(sub * SUB, SUB)], r1.at[h, sub, ob],
                 rs_s[1, h, sub, ob], rs_r[1, h, sub, ob], towards(rs_axes[h][0], step),
+            )
+
+    def first_sent(h, ob):
+        zl, row0, _ = target(h, 2, ob)
+        for sub, step in ((0, 1), (1, -1)):
+            pending.append(pltpu.make_async_remote_copy(
+                src_ref=part.at[0, zl, h, pl.ds(row0, TOK), pl.ds(sub * SUB, SUB)], dst_ref=r1.at[h, sub, ob],
+                send_sem=rs_s[1, h, sub, ob], recv_sem=rs_r[1, h, sub, ob],
+                device_id=towards(rs_axes[h][0], step), device_id_type=MESH,
             ))
 
     def second_step(h, ob):
@@ -334,16 +350,25 @@
             rs_s[4, h, sub, 0], rs_r[4, h, sub, 0], towards(rs_axes[h][1], step),
         ))
 
-    def sixth_step(h):
+    def sixth_step_early(h):
         for sub in (0, 1):
-            for late in (1, 0):
-                cols = pl.ds((sub if late == 0 else 1 - sub) * SUB, SUB)
-                arrived(r4.at[h, sub, :, cols], rs_s[4, h, sub, late], rs_r[4, h, sub, late])
+            kept = pl.ds((1 - sub) * SUB, SUB)
+            arrived(r4.at[h, sub, :, kept], rs_s[4, h, sub, 1], rs_r[4, h, sub, 1])
+
+            def add(i):
+                at = pl.ds(i, 16)
+                own[h, at, kept] = own[h, at, kept] + r4[h, sub, at, kept].astype(F32)
+
+            rows16(add)
+
+    def sixth_step(h, sub):
+        got = pl.ds(sub * SUB, SUB)
+        arrived(r4.at[h, sub, :, got], rs_s[4, h, sub, 0], rs_r[4, h, sub, 0])
 
         def add(i):
             at = pl.ds(i, 16)
-            gi_ref[at, pl.ds(h * HALF, HALF)] = (
-                own[h, at] + r4[h, 0, at].astype(F32) + r4[h, 1, at].astype(F32)
+            gi_ref[at, pl.ds(h * HALF + sub * SUB, SUB)] = (
+                own[h, at, got] + r4[h, sub, at, got].astype(F32)
             ).astype(BF)
 
         rows16(add)
@@ -359,20 +384,19 @@
         gwb[rows] = product.astype(BF)
 
     both = (0, 1)
+    pl.semaphore_wait(barrier, len(neighbours))
+    for along in (0, 1):
+        for h in both:
+            for step in (1, -1):
+                x_send_own(h, along, step)
     loads["pre"].wait()
     loads["gh"].wait()
-    for q in range(4):
+    for q in (0, 2, 1, 3):
         g_compute(q)
+        g_send(0, q, 1)
+        g_send(0, q, -1)
     loads["x0"].wait()
     loads["x1"].wait()
-    pl.semaphore_wait(barrier, len(neighbours))
-    for along in (0, 1):
-        for h in both:
-            for step in (1, -1):
-                x_send(h, 0, 0, None, along, step)
-    for q in (0, 2, 1, 3):
-        g_send(0, q, 1)
-        g_send(0, q, -1)
     for h in both:
         x_share(h, 0, 0)
     loads["w"].wait()
@@ -406,15 +430,28 @@
     for h in both:
         x_last(h, 0)
     partial(1, 1)
+    early = (x + core) % 2 == 1
+
+    def first_steps(halves):
+        for h in halves:
+            for ob in (2, 1, 3, 0):
+                first_step(h, ob)
+
+    def first_sends():
+        for h in both:
+            for ob in (2, 1, 3, 0):
+                first_sent(h, ob)
+
     for h in both:
         x_second(h, 2)
+    pl.when(early)(lambda: first_steps((0,)))
     for q in range(4):
         g_arrived(2, q)
-    for h in both:
-        partial(2, h)
-    for h in both:
-        for ob in (2, 1, 3, 0):
-            first_step(h, ob)
+    partial(2, 0)
+    pl.when(early)(lambda: first_steps((1,)))
+    partial(2, 1)
+    pl.when(jnp.logical_not(early))(lambda: first_steps(both))
+    first_sends()
     for ob in (2, 1, 3):
         for h in both:
             second_step(h, ob)
@@ -451,13 +488,15 @@
     for h in both:
         for sub in (0, 1):
             fifth_step(h, sub)
-    while len(pending) > 32:
-        pending.pop(0).wait_send()
+    drain(12)
     for h in both:
         third_step(h, 0)
     for h in both:
-        sixth_step(h)
-    drain()
+        sixth_step_early(h)
+    for sub in (0, 1):
+        for h in both:
+            sixth_step(h, sub)
+    drain(0)
 
 
 def write_out(gi, gw, gi_hbm, gw_hbm, sems):

time: 65.4 us -> 66.4 us (1.015)
  Pallas kernels: 64.7 us -> 65.5 us
    pallas_call x1, Pallas kernels: 62.4 us -> 63.2 us  [per_device(): pl.pallas_call(kernel, out_shape=(pltpu.VMEM((TOK, FEAT), BF), pltpu.VMEM...]
where the time goes in v3:
time: 66.4 us; the launch traced here: 66.3 us
  Pallas kernels  65.5 us (99%)
  between operations  0.8 us (1%)
    pallas_call x1, Pallas kernels, per_device(): pl.pallas_call(kernel, out_shape=(pltpu.VMEM((TOK, FEAT), BF), pltpu.VMEM...  63.2 us
    pallas_call x1, Pallas kernels, per_device(): pl.pallas_call(write_out, out_shape=tuple((jax.ShapeDtypeStruct(g.shape,...  2.32 us

profile of v3, /device:TPU:1, one launch (start us, length us, event | category | flops | bytes accessed | tf_op | source)
XLA Modules:
  0.0 66.3 jit_solution(10115726381946519694)
XLA Ops:
  0.6 63.2 %gelu_up_backward.1 = (bf16[48,3072]{1,0:T(8,128)(2,1)S(1)}, bf16[3072,768]{1,0:T(8,128)(2,1)S(1)}) custom-call(bf16[48,3072]{1,0:T(8,128)(2,1)} %x_hbm.1, bf16[3072,768]{1,0:T(8,128)(2,1)} %w_hbm.1, bf16[384,768]{1,0:T(8,128)(2,1)} %pre_hbm.1, bf16[384,768]{1,0:T(8,128)(2,1)} %gh_hbm.1), custom_call_target="tpu_custom_call" | custom-call | flops 14499999744 | bytes 16000000 | tf_op jit(solution)/shard_map/gelu_up_backward/pallas_call | solution.py:516
  63.8 2.3 %write_out.1 = (bf16[48,3072]{1,0:T(8,128)(2,1)}, bf16[3072,768]{1,0:T(8,128)(2,1)}) custom-call(bf16[48,3072]{1,0:T(8,128)(2,1)S(1)} %get-tuple-element.4.gi, bf16[3072,768]{1,0:T(8,128)(2,1)S(1)} %get-tuple-element.5.gw), custom_call_target="tpu_custom_call" | custom-call | tf_op jit(solution)/shard_map/write_out/pallas_call | solution.py:548

commit v4 on v3

--- a/solution.py
+++ b/solution.py
@@ -430,12 +430,17 @@
     for h in both:
         x_last(h, 0)
     partial(1, 1)
-    early = (x + core) % 2 == 1
-
-    def first_steps(halves):
+    odd = x % 2 == 1
+    lead = jnp.logical_and(core == 0, odd)
+    lead_own = jnp.logical_and(core == 0, x % 2 == 0)
+
+    def owned(h, ob):
+        return (z + (ob if h == 1 else 2)) % 2 == x // 2
+
+    def first_steps(halves, when):
         for h in halves:
             for ob in (2, 1, 3, 0):
-                first_step(h, ob)
+                pl.when(when(h, ob))(functools.partial(first_step, h, ob))
 
     def first_sends():
         for h in both:
@@ -444,13 +449,16 @@
 
     for h in both:
         x_second(h, 2)
-    pl.when(early)(lambda: first_steps((0,)))
+    first_steps(both, lambda h, ob: jnp.logical_and(lead_own, owned(h, ob)))
+    pl.when(lead)(lambda: first_steps((0,), lambda h, ob: True))
     for q in range(4):
         g_arrived(2, q)
     partial(2, 0)
-    pl.when(early)(lambda: first_steps((1,)))
+    pl.when(lead)(lambda: first_steps((1,), lambda h, ob: True))
     partial(2, 1)
-    pl.when(jnp.logical_not(early))(lambda: first_steps(both))
+    first_steps(
+        both, lambda h, ob: jnp.logical_or(core == 1, jnp.logical_and(lead_own, jnp.logical_not(owned(h, ob))))
+    )
     first_sends()
     for ob in (2, 1, 3):
         for h in both:

time: 66.4 us -> 64.3 us (0.968)
  Pallas kernels: 65.5 us -> 63.4 us
    pallas_call x1, Pallas kernels: 63.2 us -> 61.1 us  [per_device(): pl.pallas_call(kernel, out_shape=(pltpu.VMEM((TOK, FEAT), BF), pltpu.VMEM...]
where the time goes in v4:
time: 64.3 us; the launch traced here: 64.2 us
  Pallas kernels  63.4 us (99%)
  between operations  0.8 us (1%)
    pallas_call x1, Pallas kernels, per_device(): pl.pallas_call(kernel, out_shape=(pltpu.VMEM((TOK, FEAT), BF), pltpu.VMEM...  61.1 us
    pallas_call x1, Pallas kernels, per_device(): pl.pallas_call(write_out, out_shape=tuple((jax.ShapeDtypeStruct(g.shape,...  2.32 us

profile of v4, /device:TPU:1, one launch (start us, length us, event | category | flops | bytes accessed | tf_op | source)
XLA Modules:
  0.0 64.2 jit_solution(14624604424207766510)
XLA Ops:
  0.6 61.1 %gelu_up_backward.1 = (bf16[48,3072]{1,0:T(8,128)(2,1)S(1)}, bf16[3072,768]{1,0:T(8,128)(2,1)S(1)}) custom-call(bf16[48,3072]{1,0:T(8,128)(2,1)} %x_hbm.1, bf16[3072,768]{1,0:T(8,128)(2,1)} %w_hbm.1, bf16[384,768]{1,0:T(8,128)(2,1)} %pre_hbm.1, bf16[384,768]{1,0:T(8,128)(2,1)} %gh_hbm.1), custom_call_target="tpu_custom_call" | custom-call | flops 14499999744 | bytes 16000000 | tf_op jit(solution)/shard_map/gelu_up_backward/pallas_call | solution.py:524
  61.7 2.3 %write_out.1 = (bf16[48,3072]{1,0:T(8,128)(2,1)}, bf16[3072,768]{1,0:T(8,128)(2,1)}) custom-call(bf16[48,3072]{1,0:T(8,128)(2,1)S(1)} %get-tuple-element.4.gi, bf16[3072,768]{1,0:T(8,128)(2,1)S(1)} %get-tuple-element.5.gw), custom_call_target="tpu_custom_call" | custom-call | tf_op jit(solution)/shard_map/write_out/pallas_call | solution.py:556

commit v5 on v4

--- a/solution.py
+++ b/solution.py
@@ -432,7 +432,8 @@
     partial(1, 1)
     odd = x % 2 == 1
     lead = jnp.logical_and(core == 0, odd)
-    lead_own = jnp.logical_and(core == 0, x % 2 == 0)
+    lead_own = (x + core) % 2 == 0
+    last = jnp.logical_and(core == 1, x % 2 == 0)
 
     def owned(h, ob):
         return (z + (ob if h == 1 else 2)) % 2 == x // 2
@@ -457,7 +458,7 @@
     pl.when(lead)(lambda: first_steps((1,), lambda h, ob: True))
     partial(2, 1)
     first_steps(
-        both, lambda h, ob: jnp.logical_or(core == 1, jnp.logical_and(lead_own, jnp.logical_not(owned(h, ob))))
+        both, lambda h, ob: jnp.logical_or(last, jnp.logical_and(lead_own, jnp.logical_not(owned(h, ob))))
     )
     first_sends()
     for ob in (2, 1, 3):

time: 64.3 us -> 64.3 us (level)
  no operation moved by 1% of the time
where the time goes in v5:
time: 64.3 us; the launch traced here: 64.2 us
  Pallas kernels  63.4 us (99%)
  between operations  0.8 us (1%)
    pallas_call x1, Pallas kernels, per_device(): pl.pallas_call(kernel, out_shape=(pltpu.VMEM((TOK, FEAT), BF), pltpu.VMEM...  61.1 us
    pallas_call x1, Pallas kernels, per_device(): pl.pallas_call(write_out, out_shape=tuple((jax.ShapeDtypeStruct(g.shape,...  2.32 us

profile of v5, /device:TPU:1, one launch (start us, length us, event | category | flops | bytes accessed | tf_op | source)
XLA Modules:
  0.0 64.2 jit_solution(9940157543205808259)
XLA Ops:
  0.6 61.1 %gelu_up_backward.1 = (bf16[48,3072]{1,0:T(8,128)(2,1)S(1)}, bf16[3072,768]{1,0:T(8,128)(2,1)S(1)}) custom-call(bf16[48,3072]{1,0:T(8,128)(2,1)} %x_hbm.1, bf16[3072,768]{1,0:T(8,128)(2,1)} %w_hbm.1, bf16[384,768]{1,0:T(8,128)(2,1)} %pre_hbm.1, bf16[384,768]{1,0:T(8,128)(2,1)} %gh_hbm.1), custom_call_target="tpu_custom_call" | custom-call | flops 14499999744 | bytes 16000000 | tf_op jit(solution)/shard_map/gelu_up_backward/pallas_call | solution.py:525
  61.7 2.3 %write_out.1 = (bf16[48,3072]{1,0:T(8,128)(2,1)}, bf16[3072,768]{1,0:T(8,128)(2,1)}) custom-call(bf16[48,3072]{1,0:T(8,128)(2,1)S(1)} %get-tuple-element.4.gi, bf16[3072,768]{1,0:T(8,128)(2,1)S(1)} %get-tuple-element.5.gw), custom_call_target="tpu_custom_call" | custom-call | tf_op jit(solution)/shard_map/write_out/pallas_call | solution.py:557

commit v6 on v5

--- a/solution.py
+++ b/solution.py
@@ -448,10 +448,10 @@
             for ob in (2, 1, 3, 0):
                 first_sent(h, ob)
 
-    for h in both:
-        x_second(h, 2)
     first_steps(both, lambda h, ob: jnp.logical_and(lead_own, owned(h, ob)))
     pl.when(lead)(lambda: first_steps((0,), lambda h, ob: True))
+    for h in both:
+        x_second(h, 2)
     for q in range(4):
         g_arrived(2, q)
     partial(2, 0)

time: 64.3 us -> 64.5 us (level)
  no operation moved by 1% of the time
where the time goes in v6:
time: 64.5 us; the launch traced here: 64.4 us
  Pallas kernels  63.6 us (99%)
  between operations  0.8 us (1%)
    pallas_call x1, Pallas kernels, per_device(): pl.pallas_call(kernel, out_shape=(pltpu.VMEM((TOK, FEAT), BF), pltpu.VMEM...  61.3 us
    pallas_call x1, Pallas kernels, per_device(): pl.pallas_call(write_out, out_shape=tuple((jax.ShapeDtypeStruct(g.shape,...  2.32 us

profile of v6, /device:TPU:1, one launch (start us, length us, event | category | flops | bytes accessed | tf_op | source)
XLA Modules:
  0.0 64.4 jit_solution(5670242735524164611)
XLA Ops:
  0.6 61.3 %gelu_up_backward.1 = (bf16[48,3072]{1,0:T(8,128)(2,1)S(1)}, bf16[3072,768]{1,0:T(8,128)(2,1)S(1)}) custom-call(bf16[48,3072]{1,0:T(8,128)(2,1)} %x_hbm.1, bf16[3072,768]{1,0:T(8,128)(2,1)} %w_hbm.1, bf16[384,768]{1,0:T(8,128)(2,1)} %pre_hbm.1, bf16[384,768]{1,0:T(8,128)(2,1)} %gh_hbm.1), custom_call_target="tpu_custom_call" | custom-call | flops 14499999744 | bytes 16000000 | tf_op jit(solution)/shard_map/gelu_up_backward/pallas_call | solution.py:525
  61.9 2.3 %write_out.1 = (bf16[48,3072]{1,0:T(8,128)(2,1)}, bf16[3072,768]{1,0:T(8,128)(2,1)}) custom-call(bf16[48,3072]{1,0:T(8,128)(2,1)S(1)} %get-tuple-element.4.gi, bf16[3072,768]{1,0:T(8,128)(2,1)S(1)} %get-tuple-element.5.gw), custom_call_target="tpu_custom_call" | custom-call | tf_op jit(solution)/shard_map/write_out/pallas_call | solution.py:557

commit v7 on v5

--- a/solution.py
+++ b/solution.py
@@ -451,15 +451,14 @@
     for h in both:
         x_second(h, 2)
     first_steps(both, lambda h, ob: jnp.logical_and(lead_own, owned(h, ob)))
-    pl.when(lead)(lambda: first_steps((0,), lambda h, ob: True))
+    pl.when(jnp.logical_not(lead_own))(lambda: first_steps((0,), lambda h, ob: True))
     for q in range(4):
         g_arrived(2, q)
     partial(2, 0)
     pl.when(lead)(lambda: first_steps((1,), lambda h, ob: True))
     partial(2, 1)
-    first_steps(
-        both, lambda h, ob: jnp.logical_or(last, jnp.logical_and(lead_own, jnp.logical_not(owned(h, ob))))
-    )
+    pl.when(last)(lambda: first_steps((1,), lambda h, ob: True))
+    first_steps(both, lambda h, ob: jnp.logical_and(lead_own, jnp.logical_not(owned(h, ob))))
     first_sends()
     for ob in (2, 1, 3):
         for h in both:

time: 64.3 us -> 65.1 us (1.012)
  Pallas kernels: 63.4 us -> 64.2 us
    pallas_call x1, Pallas kernels: 61.1 us -> 61.8 us  [per_device(): pl.pallas_call(kernel, out_shape=(pltpu.VMEM((TOK, FEAT), BF), pltpu.VMEM...]
where the time goes in v7:
time: 65.1 us; the launch traced here: 65 us
  Pallas kernels  64.2 us (99%)
  between operations  0.8 us (1%)
    pallas_call x1, Pallas kernels, per_device(): pl.pallas_call(kernel, out_shape=(pltpu.VMEM((TOK, FEAT), BF), pltpu.VMEM...  61.8 us
    pallas_call x1, Pallas kernels, per_device(): pl.pallas_call(write_out, out_shape=tuple((jax.ShapeDtypeStruct(g.shape,...  2.32 us

profile of v7, /device:TPU:1, one launch (start us, length us, event | category | flops | bytes accessed | tf_op | source)
XLA Modules:
  0.0 65.0 jit_solution(616717783016222538)
XLA Ops:
  0.6 61.8 %gelu_up_backward.1 = (bf16[48,3072]{1,0:T(8,128)(2,1)S(1)}, bf16[3072,768]{1,0:T(8,128)(2,1)S(1)}) custom-call(bf16[48,3072]{1,0:T(8,128)(2,1)} %x_hbm.1, bf16[3072,768]{1,0:T(8,128)(2,1)} %w_hbm.1, bf16[384,768]{1,0:T(8,128)(2,1)} %pre_hbm.1, bf16[384,768]{1,0:T(8,128)(2,1)} %gh_hbm.1), custom_call_target="tpu_custom_call" | custom-call | flops 14499999744 | bytes 16000000 | tf_op jit(solution)/shard_map/gelu_up_backward/pallas_call | solution.py:524
  62.5 2.3 %write_out.1 = (bf16[48,3072]{1,0:T(8,128)(2,1)}, bf16[3072,768]{1,0:T(8,128)(2,1)}) custom-call(bf16[48,3072]{1,0:T(8,128)(2,1)S(1)} %get-tuple-element.4.gi, bf16[3072,768]{1,0:T(8,128)(2,1)S(1)} %get-tuple-element.5.gw), custom_call_target="tpu_custom_call" | custom-call | tf_op jit(solution)/shard_map/write_out/pallas_call | solution.py:556

commit v8 on v6

--- a/solution.py
+++ b/solution.py
@@ -450,11 +450,11 @@
 
     first_steps(both, lambda h, ob: jnp.logical_and(lead_own, owned(h, ob)))
     pl.when(lead)(lambda: first_steps((0,), lambda h, ob: True))
-    for h in both:
-        x_second(h, 2)
     for q in range(4):
         g_arrived(2, q)
     partial(2, 0)
+    for h in both:
+        x_second(h, 2)
     pl.when(lead)(lambda: first_steps((1,), lambda h, ob: True))
     partial(2, 1)
     first_steps(

time: 64.5 us -> 64.4 us (level)
  no operation moved by 1% of the time
where the time goes in v8:
time: 64.4 us; the launch traced here: 64.3 us
  Pallas kernels  63.5 us (99%)
  between operations  0.8 us (1%)
    pallas_call x1, Pallas kernels, per_device(): pl.pallas_call(kernel, out_shape=(pltpu.VMEM((TOK, FEAT), BF), pltpu.VMEM...  61.2 us
    pallas_call x1, Pallas kernels, per_device(): pl.pallas_call(write_out, out_shape=tuple((jax.ShapeDtypeStruct(g.shape,...  2.32 us

profile of v8, /device:TPU:1, one launch (start us, length us, event | category | flops | bytes accessed | tf_op | source)
XLA Modules:
  0.0 64.3 jit_solution(3754345613800862256)
XLA Ops:
  0.6 61.2 %gelu_up_backward.1 = (bf16[48,3072]{1,0:T(8,128)(2,1)S(1)}, bf16[3072,768]{1,0:T(8,128)(2,1)S(1)}) custom-call(bf16[48,3072]{1,0:T(8,128)(2,1)} %x_hbm.1, bf16[3072,768]{1,0:T(8,128)(2,1)} %w_hbm.1, bf16[384,768]{1,0:T(8,128)(2,1)} %pre_hbm.1, bf16[384,768]{1,0:T(8,128)(2,1)} %gh_hbm.1), custom_call_target="tpu_custom_call" | custom-call | flops 14499999744 | bytes 16000000 | tf_op jit(solution)/shard_map/gelu_up_backward/pallas_call | solution.py:525
  61.8 2.3 %write_out.1 = (bf16[48,3072]{1,0:T(8,128)(2,1)}, bf16[3072,768]{1,0:T(8,128)(2,1)}) custom-call(bf16[48,3072]{1,0:T(8,128)(2,1)S(1)} %get-tuple-element.4.gi, bf16[3072,768]{1,0:T(8,128)(2,1)S(1)} %get-tuple-element.5.gw), custom_call_target="tpu_custom_call" | custom-call | tf_op jit(solution)/shard_map/write_out/pallas_call | solution.py:557
